TPU v7x, 32 devices: a whole 2x2x4 slice. The times are simulated.
32 devices in a mesh: role: 2 (over core), slab: 16 (over z, y, x).
Axes of the slice: x: 2, y: 2, z: 4, core: 2. Of those that a mesh axis runs over, the one named last changes fastest.
Arguments:
- velocity: float32 [4, 32, 128, 256], P(None, 'slab', 'role'), may hold values from -18 to 18
- basis: bfloat16 [256, 32, 128, 256], P(None, 'slab', 'role'), may hold values from -1 to 1, as said below
- mean_flow: float32 [128], replicated, may hold values from 0.2 to 2
- shear: float32 [128], replicated, may hold values from -1 to 1
Outputs:
- advanced: float32 [4, 32, 128, 256], P(None, 'slab', 'role')
- coeffs: float32 [256, 8], replicated
- rfactor: float32 [8, 8], replicated
- directions: float32 [8, 32, 128, 256], P(None, 'slab', 'role')
Inputs may be any that keep to these rules, and one draw needn't show every extreme that they name: Every column of the basis has length within a few percent of one, and distinct columns are nearly orthogonal.
All inputs are finite; a program needn't handle non-finite values.
Results may differ from a plain program's by a relative error of at most 0.00035.
The roundings to bfloat16 on the way count: a program that leaves them out, or rounds other values in their place, can miss the bound.
Values sent between devices are 32-bit elements; how exact they have to be, the bound alone decides.
A program may use at most 128 MiB of HBM per device.

v0:
```python
import jax
import jax.numpy as jnp
from jax import lax
from jax.sharding import PartitionSpec as P

viscosity = 0.1
time_step = 0.4


def extended(cells, sides, width, closed):
    for axis, dim in sides:
        count = lax.axis_size(axis)
        ends = count if closed else count - 1
        head = lax.slice_in_dim(cells, 0, width, axis=dim)
        tail = lax.slice_in_dim(cells, cells.shape[dim] - width, cells.shape[dim], axis=dim)
        cells = jnp.concatenate(
            [
                lax.ppermute(tail, axis, [(i, (i + 1) % count) for i in range(ends)]),
                cells,
                lax.ppermute(head, axis, [((i + 1) % count, i) for i in range(ends)]),
            ],
            axis=dim,
        )
    return cells


def offset_slice(padded, offset, dimension, length):
    return lax.slice_in_dim(padded, 2 + offset, 2 + offset + length, axis=dimension)


def second_diff(padded, center, dimension, length):
    return (
        -offset_slice(padded, 2, dimension, length)
        + 16.0 * offset_slice(padded, 1, dimension, length)
        - 30.0 * center
        + 16.0 * offset_slice(padded, -1, dimension, length)
        - offset_slice(padded, -2, dimension, length)
    ) / 12.0


def stencil(center, xpadded, ypadded, flow_rows, shear_rows):
    nx_loc = center.shape[1]
    ny_loc = center.shape[2]
    nz_loc = center.shape[3]
    zpadded = jnp.concatenate([center[..., -2:], center, center[..., :2]], axis=3)
    first_x = (
        -offset_slice(xpadded, 2, 1, nx_loc)
        + 8.0 * offset_slice(xpadded, 1, 1, nx_loc)
        - 8.0 * offset_slice(xpadded, -1, 1, nx_loc)
        + offset_slice(xpadded, -2, 1, nx_loc)
    ) / 12.0
    laplace = (
        second_diff(xpadded, center, 1, nx_loc)
        + second_diff(ypadded, center, 2, ny_loc)
        + second_diff(zpadded, center, 3, nz_loc)
    )
    profile = flow_rows[None, None, :, None]
    result = -profile * first_x + viscosity * laplace
    shear_term = shear_rows[None, None, :, None] * center[1:2]
    return jnp.concatenate([result[:1] - shear_term, result[1:]], axis=0)


def segmented_tendency(center, flow_rows, shear_rows):
    xpadded = extended(center, (("slab", 1),), 2, True)
    ypadded = extended(center, (("role", 2),), 2, False)
    return stencil(center, xpadded, ypadded, flow_rows, shear_rows)


def on_device(velocity, basis, mean_flow, shear):
    ny_loc = velocity.shape[2]
    role_index = lax.axis_index("role")
    flow_rows = lax.dynamic_slice_in_dim(mean_flow, role_index * ny_loc, ny_loc)
    shear_rows = lax.dynamic_slice_in_dim(shear, role_index * ny_loc, ny_loc)
    tend_zero = segmented_tendency(velocity, flow_rows, shear_rows)
    segment_one = velocity + time_step * (8.0 / 15.0) * tend_zero
    tend_one = segmented_tendency(segment_one, flow_rows, shear_rows)
    advanced = segment_one + time_step * (5.0 / 12.0 * tend_one - 17.0 / 60.0 * tend_zero)
    snapshots = jnp.concatenate([segment_one, advanced], axis=0)
    flat_snaps = snapshots.reshape(snapshots.shape[0], -1)
    snaps_bf = flat_snaps.astype(jnp.bfloat16)
    basis_rows = basis.reshape(basis.shape[0], -1)
    partial_proj = jnp.einsum("km,sm->ks", basis_rows, snaps_bf, preferred_element_type=jnp.float32)
    coeffs = lax.psum(partial_proj, ("role", "slab"))
    coeffs_bf = coeffs.astype(jnp.bfloat16)
    residual = flat_snaps - jnp.einsum(
        "ks,km->sm", coeffs_bf, basis_rows, preferred_element_type=jnp.float32
    )
    local_gram = jnp.dot(residual, residual.T, precision=lax.Precision.HIGHEST)
    total_gram = lax.psum(local_gram, ("role", "slab"))
    lower_factor = jnp.linalg.cholesky(total_gram)
    directions = jax.scipy.linalg.solve_triangular(lower_factor, residual, lower=True)
    return (advanced, coeffs, lower_factor.T, directions.reshape(snapshots.shape))


def solution(mesh):
    return jax.shard_map(
        on_device,
        mesh=mesh,
        in_specs=(P(None, "slab", "role", None), P(None, "slab", "role", None), P(), P()),
        out_specs=(P(None, "slab", "role", None), P(), P(), P(None, "slab", "role", None)),
        check_vma=False,
    )
```

profile of v0, /device:TPU:0, one launch (start us, length us, event | category | flops | bytes accessed | tf_op | source)
XLA Modules:
  0.0 182.0 jit_solution(12322529143654965869)
XLA Ops:
  0.6 1.4 copy.23
  2.0 3.0 %collective-permute-start.1 = (f32[4,2,64,256]{3,0,2,1:T(4,128)S(1)}, f32[4,2,64,256]{3,0,2,1:T(4,128)S(1)}, u32[]{:S(2)}, u32[]{:S(2)}) collective-permute-start(f32[4,2,64,256]{3,0,2,1:T(4,128)S(1)} %copy.23), channel_id=1, source_target_pairs={{0,1},{1,2},{2,3},{3,4},{4,5},{5,6},{6,7},{7,8},{8,9},{9,10},{10,1... | collective-permute-start | bytes 1572872 | tf_op jit(solution)/shard_map/ppermute | solution.py:18
  5.0 4.1 %collective-permute-start = (f32[4,2,64,256]{3,0,2,1:T(4,128)S(1)}, f32[4,2,64,256]{3,0,2,1:T(4,128)S(1)}, u32[]{:S(2)}, u32[]{:S(2)}) collective-permute-start(f32[4,2,64,256]{3,0,2,1:T(4,128)S(1)} %copy.23), channel_id=1, source_target_pairs={{1,0},{2,1},{3,2},{4,3},{5,4},{6,5},{7,6},{8,7},{9,8},{10,9},{11,1... | collective-permute-start | bytes 1572872 | tf_op jit(solution)/shard_map/ppermute | solution.py:20
  9.1 1.3 collective-permute-start.2
  10.4 3.0 %collective-permute-start.3 = (f32[4,2,2,256]{3,0,2,1:T(4,128)S(1)}, f32[4,2,2,256]{3,0,2,1:T(4,128)S(1)}, u32[]{:S(2)}, u32[]{:S(2)}) collective-permute-start(f32[4,2,2,256]{3,0,2,1:T(4,128)S(1)} %get-tuple-element.13), channel_id=1, source_target_pairs={{0,16},{1,17},{2,18},{3,19},{4,20},{5,21},{6,22},{7,23},{8,24},{9,... | collective-permute-start | bytes 49160 | tf_op jit(solution)/shard_map/ppermute | solution.py:18
  14.3 1.0 slice_multiply_fusion.3
  16.1 1.5 constant_dynamic-update-slice_fusion.1
  17.6 9.9 %collective-permute-done.1 = f32[4,2,64,256]{3,0,2,1:T(4,128)S(1)} collective-permute-done((f32[4,2,64,256]{3,0,2,1:T(4,128)S(1)}, f32[4,2,64,256]{3,0,2,1:T(4,128)S(1)}, u32[]{:S(2)}, u32[]{:S(2)}) %collective-permute-start.1) | collective-permute-done | bytes 524320 | tf_op jit(solution)/shard_map/ppermute | solution.py:18
  27.4 1.9 %collective-permute-done = f32[4,2,64,256]{3,0,2,1:T(4,128)S(1)} collective-permute-done((f32[4,2,64,256]{3,0,2,1:T(4,128)S(1)}, f32[4,2,64,256]{3,0,2,1:T(4,128)S(1)}, u32[]{:S(2)}, u32[]{:S(2)}) %collective-permute-start) | collective-permute-done | bytes 524320 | tf_op jit(solution)/shard_map/ppermute | solution.py:20
  29.4 1.9 %fusion.31 = f32[4,2,64,256]{3,0,2,1:T(4,128)S(1)} fusion(f32[4,2,64,2]{3,0,2,1:T(4,128)S(1)} %get-tuple-element.17, f32[4,2,64,256]{3,0,2,1:T(4,128)S(1)} %copy.23, f32[4,2,64,2]{3,0,2,1:T(4,128)S(1)} %get-tuple-element.16, f32[4,2,66,256]{3,0,2,1:T(4,128)S(1)} %get-tuple-element.15, f32[4,2,66,256]{3,0,2,1:T(4,128)S(1)} %constant_dynamic-update-slice_fusion, ...), kind=kLoop, calls=%fused_computation.43 | loop fusion | flops 4980736 | bytes 4202752 | tf_op jit(solution)/shard_map/add | solution.py:58
  31.7 1.6 multiply_add_fusion
  33.3 1.5 collective-permute-start.5
  34.8 4.1 %collective-permute-start.4 = (f32[4,2,64,256]{3,0,2,1:T(4,128)S(1)}, f32[4,2,64,256]{3,0,2,1:T(4,128)S(1)}, u32[]{:S(2)}, u32[]{:S(2)}) collective-permute-start(f32[4,2,64,256]{3,0,2,1:T(4,128)S(1)} %multiply_add_fusion), channel_id=1, source_target_pairs={{1,0},{2,1},{3,2},{4,3},{5,4},{6,5},{7,6},{8,7},{9,8},{10,9},{11,1... | collective-permute-start | bytes 1572872 | tf_op jit(solution)/shard_map/ppermute | solution.py:20
  39.0 17.9 %copy.34 = bf16[32,8,128,256]{3,1,2,0:T(8,128)(2,1)} copy(bf16[32,8,128,256]{3,2,1,0:T(8,128)(2,1)} %bitcast.33) | data formatting | bytes 33554432
  56.9 1.3 collective-permute-start.6
  58.1 3.2 %collective-permute-start.7 = (f32[4,2,2,256]{3,0,2,1:T(4,128)S(1)}, f32[4,2,2,256]{3,0,2,1:T(4,128)S(1)}, u32[]{:S(2)}, u32[]{:S(2)}) collective-permute-start(f32[4,2,2,256]{3,0,2,1:T(4,128)S(1)} %get-tuple-element.11), channel_id=1, source_target_pairs={{0,16},{1,17},{2,18},{3,19},{4,20},{5,21},{6,22},{7,23},{8,24},{9,... | collective-permute-start | bytes 49160 | tf_op jit(solution)/shard_map/ppermute | solution.py:18
  62.0 2.6 %fusion.12 = f32[4,2,64,256]{3,0,2,1:T(4,128)S(1)} fusion(f32[4,2,2,256]{3,0,2,1:T(4,128)S(1)} %collective-permute-done.7, f32[4,2,64,256]{3,0,2,1:T(4,128)S(1)} %multiply_add_fusion, f32[4,2,2,256]{3,0,2,1:T(4,128)S(1)} %collective-permute-done.6, f32[4,2,64,2]{3,0,2,1:T(4,128)S(1)} %get-tuple-element.9, f32[4,2,64,2]{3,0,2,1:T(4,128)S(1)} %get-tuple-element.8, ...), kind=kLoop, calls=%fused_computation.24 | loop fusion | flops 5505024 | bytes 2138368 | tf_op jit(solution)/shard_map/add | solution.py:58
  65.9 20.8 %fusion.2 = f32[256,8]{0,1:T(8,128)S(1)} fusion(bf16[256,2,64,256]{3,2,1,0:T(8,128)(2,1)} %param.5, f32[4,2,64,256]{3,0,2,1:T(4,128)S(1)} %fusion.47, f32[4,2,64,256]{3,0,2,1:T(4,128)S(1)} %multiply_add_fusion), kind=kOutput, calls=%fused_computation.3 | convolution fusion | flops 135266304 | bytes 17833984 | tf_op jit(solution)/shard_map/km,sm->ks/dot_general | solution.py:82
  87.8 37.8 %psum.14 = f32[256,8]{0,1:T(8,128)S(1)} all-reduce(f32[256,8]{0,1:T(8,128)S(1)} %fusion.2), channel_id=1, replica_groups=mesh['role'=2,'slab'=16] {'role','slab'}, use_global_device_ids=true, to_apply=%region_0.0 | all-reduce | flops 2048 | bytes 16384 | tf_op jit(solution)/shard_map/psum | solution.py:83
  125.5 8.0 %convolution_subtract_fusion = f32[8,32768]{1,0:T(8,128)S(1)} fusion(f32[8,32768]{1,0:T(8,128)S(1)} %bitcast.36, bf16[256,32768]{1,0:T(8,128)(2,1)} %bitcast.34, f32[256,8]{0,1:T(8,128)S(1)} %psum.14), kind=kOutput, calls=%fused_computation | convolution fusion | flops 134481920 | bytes 18882560 | tf_op jit(solution)/shard_map/ks,km->sm/dot_general | solution.py:85
  133.6 2.3 %fusion.59 = f32[8,8]{0,1:T(8,128)S(1)} fusion(f32[8,32768]{1,0:T(8,128)S(1)} %convolution_subtract_fusion), kind=kOutput, calls=%fused_computation.104 | convolution fusion | flops 25165824 | bytes 1048832 | tf_op jit(solution)/shard_map/dot_general | solution.py:88
  135.9 40.3 %psum.15 = f32[8,8]{0,1:T(8,128)S(1)} all-reduce(f32[8,8]{0,1:T(8,128)S(1)} %fusion.59), channel_id=1, replica_groups=mesh['role'=2,'slab'=16] {'role','slab'}, use_global_device_ids=true, to_apply=%region_1.0 | all-reduce | flops 64 | bytes 512 | tf_op jit(solution)/shard_map/psum | solution.py:89
  179.0 1.0 fusion.50
  180.0 1.3 copy.30
  (33 shorter events, 8.4 us)
Async XLA Ops:
  2.0 25.4 %collective-permute-start.1 = (f32[4,2,64,256]{3,0,2,1:T(4,128)S(1)}, f32[4,2,64,256]{3,0,2,1:T(4,128)S(1)}, u32[]{:S(2)}, u32[]{:S(2)}) collective-permute-start(f32[4,2,64,256]{3,0,2,1:T(4,128)S(1)} %copy.23), channel_id=1, source_target_pairs={{0,1},{1,2},{2,3},{3,4},{4,5},{5,6},{6,7},{7,8},{8,9},{9,10},{10,1... | collective-permute-start | bytes 1572872 | tf_op jit(solution)/shard_map/ppermute | solution.py:18
  5.0 24.4 %collective-permute-start = (f32[4,2,64,256]{3,0,2,1:T(4,128)S(1)}, f32[4,2,64,256]{3,0,2,1:T(4,128)S(1)}, u32[]{:S(2)}, u32[]{:S(2)}) collective-permute-start(f32[4,2,64,256]{3,0,2,1:T(4,128)S(1)} %copy.23), channel_id=1, source_target_pairs={{1,0},{2,1},{3,2},{4,3},{5,4},{6,5},{7,6},{8,7},{9,8},{10,9},{11,1... | collective-permute-start | bytes 1572872 | tf_op jit(solution)/shard_map/ppermute | solution.py:20
  9.1 8.5 %collective-permute-start.2 = (f32[4,2,2,256]{3,0,2,1:T(4,128)S(1)}, f32[4,2,2,256]{3,0,2,1:T(4,128)S(1)}, u32[]{:S(2)}, u32[]{:S(2)}) collective-permute-start(f32[4,2,2,256]{3,0,2,1:T(4,128)S(1)} %get-tuple-element.12), channel_id=1, source_target_pairs={{16,0},{17,1},{18,2},{19,3},{20,4},{21,5},{22,6},{23,7},{24,8},{25... | collective-permute-start | bytes 49160 | tf_op jit(solution)/shard_map/ppermute | solution.py:20
  10.4 5.7 %collective-permute-start.3 = (f32[4,2,2,256]{3,0,2,1:T(4,128)S(1)}, f32[4,2,2,256]{3,0,2,1:T(4,128)S(1)}, u32[]{:S(2)}, u32[]{:S(2)}) collective-permute-start(f32[4,2,2,256]{3,0,2,1:T(4,128)S(1)} %get-tuple-element.13), channel_id=1, source_target_pairs={{0,16},{1,17},{2,18},{3,19},{4,20},{5,21},{6,22},{7,23},{8,24},{9,... | collective-permute-start | bytes 49160 | tf_op jit(solution)/shard_map/ppermute | solution.py:18
  33.3 28.7 %collective-permute-start.5 = (f32[4,2,64,256]{3,0,2,1:T(4,128)S(1)}, f32[4,2,64,256]{3,0,2,1:T(4,128)S(1)}, u32[]{:S(2)}, u32[]{:S(2)}) collective-permute-start(f32[4,2,64,256]{3,0,2,1:T(4,128)S(1)} %multiply_add_fusion), channel_id=1, source_target_pairs={{0,1},{1,2},{2,3},{3,4},{4,5},{5,6},{6,7},{7,8},{8,9},{9,10},{10,1... | collective-permute-start | bytes 1572872 | tf_op jit(solution)/shard_map/ppermute | solution.py:18
  34.8 27.2 %collective-permute-start.4 = (f32[4,2,64,256]{3,0,2,1:T(4,128)S(1)}, f32[4,2,64,256]{3,0,2,1:T(4,128)S(1)}, u32[]{:S(2)}, u32[]{:S(2)}) collective-permute-start(f32[4,2,64,256]{3,0,2,1:T(4,128)S(1)} %multiply_add_fusion), channel_id=1, source_target_pairs={{1,0},{2,1},{3,2},{4,3},{5,4},{6,5},{7,6},{8,7},{9,8},{10,9},{11,1... | collective-permute-start | bytes 1572872 | tf_op jit(solution)/shard_map/ppermute | solution.py:20
  39.0 26.0 %copy-start = (f32[4,2,64,256]{3,2,1,0:T(8,128)S(1)}, f32[4,2,64,256]{3,2,1,0:T(8,128)}, u32[]{:S(2)}) copy-start(f32[4,2,64,256]{3,2,1,0:T(8,128)} %param.4) | copy-start | bytes 1572868
  56.9 4.7 %collective-permute-start.6 = (f32[4,2,2,256]{3,0,2,1:T(4,128)S(1)}, f32[4,2,2,256]{3,0,2,1:T(4,128)S(1)}, u32[]{:S(2)}, u32[]{:S(2)}) collective-permute-start(f32[4,2,2,256]{3,0,2,1:T(4,128)S(1)} %get-tuple-element.10), channel_id=1, source_target_pairs={{16,0},{17,1},{18,2},{19,3},{20,4},{21,5},{22,6},{23,7},{24,8},{25... | collective-permute-start | bytes 49160 | tf_op jit(solution)/shard_map/ppermute | solution.py:20
  58.1 3.9 %collective-permute-start.7 = (f32[4,2,2,256]{3,0,2,1:T(4,128)S(1)}, f32[4,2,2,256]{3,0,2,1:T(4,128)S(1)}, u32[]{:S(2)}, u32[]{:S(2)}) collective-permute-start(f32[4,2,2,256]{3,0,2,1:T(4,128)S(1)} %get-tuple-element.11), channel_id=1, source_target_pairs={{0,16},{1,17},{2,18},{3,19},{4,20},{5,21},{6,22},{7,23},{8,24},{9,... | collective-permute-start | bytes 49160 | tf_op jit(solution)/shard_map/ppermute | solution.py:18
  125.5 56.4 %copy-start.1 = (f32[256,8]{0,1:T(8,128)}, f32[256,8]{0,1:T(8,128)S(1)}, u32[]{:S(2)}) copy-start(f32[256,8]{0,1:T(8,128)S(1)} %psum.14) | copy-start | bytes 24580
where the time goes:
time: 183 us; the launch traced here: 182 us
  blocking collectives  78.1 us (43%)
  matrix products  32.2 us (18%)
  local copies, waits for them, and re-layouts  25.1 us (14%)
  starting transfers between devices  21.5 us (12%)
  waiting for transfers between devices  12.2 us (7%)
  other arithmetic  12 us (7%)
    psum x1, blocking collectives, on_device(): total_gram = lax.psum(local_gram, ('role', 'slab'))  40.3 us
    psum x1, blocking collectives, on_device(): coeffs = lax.psum(partial_proj, ('role', 'slab'))  37.8 us
    unnamed x11, local copies, waits for them, and re-layouts  23.6 us
    dot_general x1, matrix products, on_device(): jnp.einsum('km,sm->ks', basis_rows, snaps_bf, preferred_element_type=jnp....  20.8 us
    ppermute x4, starting transfers between devices, extended(): lax.ppermute(tail, axis, [(i, (i + 1) % count) for i in range(ends)])  10.8 us
    ppermute x4, starting transfers between devices, extended(): lax.ppermute(head, axis, [((i + 1) % count, i) for i in range(ends)])  10.7 us
    ppermute x4, waiting for transfers between devices, extended(): lax.ppermute(tail, axis, [(i, (i + 1) % count) for i in range(ends)])  10.3 us
    dot_general x1, matrix products, on_device(): jnp.einsum('ks,km->sm', coeffs_bf, basis_rows, preferred_element_type=jnp...  8.05 us
  transfers between devices with their start and end apart: 8, of which 3 were waited for; matrix products, arithmetic and copies ran while one was open for 12% of the time, Pallas kernels for 0%

commit v1 on v0

v1 whole, which is shorter than its diff:
```python
import functools

import jax
import jax.numpy as jnp
from jax import lax
from jax.experimental import pallas as pl
from jax.experimental.pallas import tpu as pltpu
from jax.sharding import PartitionSpec as P

viscosity = 0.1
time_step = 0.4
MESH = pl.DeviceIdType.MESH
HIGHEST = lax.Precision.HIGHEST
T = 16


def iota(shape, dim):
    return lax.broadcasted_iota(jnp.int32, shape, dim)


def same_row(rows, cols):
    return (iota((rows, cols), 0) % T) == (iota((rows, cols), 1) % T)


def nt_dot(a, b, precision=None):
    return lax.dot_general(
        a, b, (((1,), (1,)), ((), ())), precision=precision, preferred_element_type=jnp.float32
    )


def kernel(groups, v_ref, basis_ref, flow_ref, shear_ref,
           adv_ref, coef_ref, r_ref, dir_ref,
           bas, s1, halo, yh, yx, prof, tend, sbf, racc, cbig, wres,
           pa, pb, ga, gb,
           bas_sem, part_s, part_r, fwd_s, fwd_r, z_s, z_r, y_s, y_r,
           pa_s, pa_r, pb_s, pb_r, ga_s, ga_r, gb_s, gb_r):
    nf, nx, ny, nz = v_ref.shape
    nk = bas.shape[0]
    nyg = ny // T
    cells = nx * nyg
    role = lax.axis_index("role")
    slab = lax.axis_index("slab")
    j = slab % 4
    g = slab // 4
    base = g * 4
    partner = base + j + 1 - 2 * (j % 2)
    across = base + (j + 2) % 4
    zto = ((g + 1 - 2 * (j // 2) + groups) % groups) * 4 + j
    lslot = (1 - j % 2) * (2 - j // 2)
    rslot = (j % 2) * (1 + j // 2)
    me8 = role * 4 + j

    basis_copy = pltpu.make_async_copy(basis_ref, bas, bas_sem)
    basis_copy.start()

    barrier = pltpu.get_barrier_semaphore()
    plane_peers = []
    for o in range(1, 8):
        p = (me8 + o) % 8
        plane_peers.append((p, (p // 4, base + p % 4)))
    group_peers = []
    for o in range(1, groups):
        p = (g + o) % groups
        group_peers.append((p, (role, p * 4 + j)))
    for _, dev in plane_peers + group_peers:
        pl.semaphore_signal(barrier, inc=1, device_id=dev, device_id_type=MESH)
    pl.semaphore_wait(barrier, 6 + groups)

    def remote(src, dst, ss, rs, dev):
        return pltpu.make_async_remote_copy(
            src_ref=src, dst_ref=dst, send_sem=ss, recv_sem=rs, device_id=dev, device_id_type=MESH
        )

    chunks = 2 * nf * nx

    def where_of(c):
        e, rest = divmod(c, nf * nx)
        return e, rest // nx, rest % nx

    def part_copy(c):
        e, f, x = where_of(c)
        src = (v_ref if e == 0 else s1).at[f, x]
        return remote(src, halo.at[e, 0, f, x], part_s.at[c], part_r.at[c], (role, partner))

    def fwd_copy(c):
        e, f, x = where_of(c)
        return remote(halo.at[e, 0, f, x], halo.at[e, 1, f, x], fwd_s.at[c], fwd_r.at[c], (role, across))

    def z_copy(c):
        e, f, x = where_of(c)
        return remote(halo.at[e, 1, f, x], halo.at[e, 2, f, x], z_s.at[c], z_r.at[c], (role, zto))

    row0 = pl.multiple_of((1 - role) * (ny - 8), 8)

    def y_copy(e, f):
        src = (v_ref if e == 0 else s1).at[f, :, pl.ds(row0, 8), :]
        i = e * nf + f
        return remote(src, yh.at[e, f], y_s.at[i], y_r.at[i], (1 - role, slab))

    for c in range(nf * nx):
        part_copy(c).start()
    for f in range(nf):
        y_copy(0, f).start()

    total = flow_ref.shape[1]
    pick = iota((ny, total), 1) == iota((ny, total), 0) + role * ny
    for i, ref in enumerate((flow_ref, shear_ref)):
        col = jnp.sum(jnp.where(pick, ref[...], 0.0), axis=1, keepdims=True)
        prof[i] = jnp.broadcast_to(col, (ny, nz))
    role_f = role.astype(jnp.float32)

    def tendency(e, f):
        src = v_ref if e == 0 else s1
        layers = [halo[e, lslot, f, 0], halo[e, lslot, f, 1], src[f, 0], src[f, 1],
                  halo[e, rslot, f, 0], halo[e, rslot, f, 1]]
        out = []
        for x in range(nx):
            l2, l1, q, r1, r2 = layers[x:x + 5]
            edge = yh[e, f, x]
            yx[x, 0:8, :] = edge * role_f
            yx[x, 8:8 + ny, :] = q
            yx[x, 8 + ny:16 + ny, :] = edge * (1.0 - role_f)
            near = (l1 + r1) + (yx[x, 7:7 + ny, :] + yx[x, 9:9 + ny, :])
            far = (l2 + r2) + (yx[x, 6:6 + ny, :] + yx[x, 10:10 + ny, :])
            near = near + (pltpu.roll(q, 1, 1) + pltpu.roll(q, nz - 1, 1))
            far = far + (pltpu.roll(q, 2, 1) + pltpu.roll(q, nz - 2, 1))
            first = (8.0 * (r1 - l1) - (r2 - l2)) * (1.0 / 12.0)
            lap = (16.0 * near - far - 90.0 * q) * (viscosity / 12.0)
            res = lap - prof[0] * first
            if f == 0:
                res = res - prof[1] * src[1, x]
            out.append(res)
        return out

    def keep_rounded(half, f, x, vals):
        for yg in range(nyg):
            sbf[half, x * nyg + yg, f * T:(f + 1) * T, :] = vals[yg * T:(yg + 1) * T, :].astype(jnp.bfloat16)

    def project(half, kb):
        acc = None
        for i in range(cells):
            x, y0 = i // nyg, (i % nyg) * T
            lhs = bas[pl.ds(kb * T, T), x, y0:y0 + T, :].reshape(T * T, nz)
            d = nt_dot(lhs, sbf[half, i])
            acc = d if acc is None else acc + d
        acc = jnp.where(same_row(T * T, nf * T), acc, 0.0)
        racc[half, pl.ds(pl.multiple_of(kb * T, T), T), :] = jnp.sum(acc.reshape(T, T, nf * T), axis=1)

    def project_range(half, lo, hi):
        def body(kb, carry):
            project(half, kb)
            return carry
        lax.fori_loop(lo, hi, body, 0)

    nkb = nk // T
    edge_chip = j % 3 == 0
    done_kb = 0
    for t in range(chunks + 2):
        if t < chunks:
            part_copy(t).wait_recv()
            fwd_copy(t).start()
        if 0 <= t - 1 < chunks:
            fwd_copy(t - 1).wait_recv()

            @pl.when(edge_chip)
            def _():
                z_copy(t - 1).start()
        if t - 2 >= 0:
            c = t - 2

            @pl.when(edge_chip)
            def _():
                z_copy(c).wait_recv()
            e, f, x = where_of(c)
            if x == nx - 1:
                y_copy(e, f).wait_recv()
                tens = tendency(e, f)
                if e == 0:
                    for xx in range(nx):
                        val = v_ref[f, xx] + (time_step * 8.0 / 15.0) * tens[xx]
                        s1[f, xx] = val
                        tend[f, xx] = tens[xx]
                        keep_rounded(0, f, xx, val)
                    for xx in range(nx):
                        part_copy(nf * nx + f * nx + xx).start()
                    y_copy(1, f).start()
                else:
                    for xx in range(nx):
                        val = s1[f, xx] + (
                            (time_step * 5.0 / 12.0) * tens[xx] - (time_step * 17.0 / 60.0) * tend[f, xx]
                        )
                        adv_ref[f, xx] = val
                        keep_rounded(1, f, xx, val)
        first = nf * nx + 2
        if t >= first:
            if t == first:
                basis_copy.wait()
            upto = ((t - first + 1) * nkb) // (chunks + 2 - first)
            project_range(0, done_kb, upto)
            done_kb = upto
    project_range(1, 0, nkb)

    pt = None
    for half in range(2):
        pick8 = (iota((8, nf * T), 0) - nf * half == iota((8, nf * T), 1) // T).astype(jnp.float32)
        d = nt_dot(pick8, racc[half], HIGHEST)
        pt = d if pt is None else pt + d

    def all_sum(val, a, b, a_s, a_r, b_s, b_r):
        a[me8] = val
        for p, dev in plane_peers:
            remote(a.at[me8], a.at[me8], a_s.at[p], a_r.at[me8], dev).start()
        for p, dev in plane_peers:
            remote(a.at[p], a.at[p], a_s.at[p], a_r.at[p], dev).wait_recv()
        val = a[0]
        for i in range(1, 8):
            val = val + a[i]
        b[g] = val
        for p, dev in group_peers:
            remote(b.at[g], b.at[g], b_s.at[p], b_r.at[g], dev).start()
        for p, dev in group_peers:
            remote(b.at[p], b.at[p], b_s.at[p], b_r.at[p], dev).wait_recv()
        val = b[0]
        for i in range(1, groups):
            val = val + b[i]
        return val

    def all_sum_sent(a, b, a_s, a_r, b_s, b_r):
        for p, dev in plane_peers:
            remote(a.at[me8], a.at[me8], a_s.at[p], a_r.at[me8], dev).wait_send()
        for p, dev in group_peers:
            remote(b.at[g], b.at[g], b_s.at[p], b_r.at[g], dev).wait_send()

    coeffs = all_sum(pt, pa, pb, pa_s, pa_r, pb_s, pb_r)
    coef_ref[...] = coeffs
    cb = coeffs.astype(jnp.bfloat16)

    ns = 2 * nf

    def spread(kb, carry):
        rep = (iota((nk, T * T), 0) == kb * T + iota((nk, T * T), 1) // T)
        rep = rep.astype(jnp.float32).astype(jnp.bfloat16)
        row = jnp.dot(cb, rep, preferred_element_type=jnp.float32)
        full = jnp.broadcast_to(row[:, None, :], (ns, T, T * T)).reshape(ns * T, T * T)
        cbig[kb] = jnp.where(same_row(ns * T, T * T), full, 0.0).astype(jnp.bfloat16)
        return carry

    lax.fori_loop(0, nkb, spread, 0)

    def residual(i, gram):
        x = i // nyg
        y0 = pl.multiple_of((i % nyg) * T, T)
        acc = None
        for kb in range(nkb):
            rhs = bas[kb * T:(kb + 1) * T, x, pl.ds(y0, T), :].reshape(T * T, nz)
            d = jnp.dot(cbig[kb], rhs, preferred_element_type=jnp.float32)
            acc = d if acc is None else acc + d
        snap = jnp.concatenate(
            [s1[:, x, pl.ds(y0, T), :].reshape(nf * T, nz), adv_ref[:, x, pl.ds(y0, T), :].reshape(nf * T, nz)],
            axis=0,
        )
        w = snap - acc
        wres[i] = w
        return gram + nt_dot(w, w, HIGHEST)

    gram = lax.fori_loop(0, cells, residual, jnp.zeros((ns * T, ns * T), jnp.float32))
    gram = jnp.where(same_row(ns * T, ns * T), gram, 0.0)
    gram = jnp.sum(gram.reshape(ns, T, ns * T), axis=1)
    gram = all_sum(gram, ga, gb, ga_s, ga_r, gb_s, gb_r)

    wide = ns * T
    fold = (iota((wide, wide), 0) // T == iota((wide, wide), 1)).astype(jnp.float32)
    rows, cols = iota((ns, wide), 0), iota((ns, wide), 1)
    aug = jnp.dot(gram, fold, precision=HIGHEST, preferred_element_type=jnp.float32)
    aug = jnp.where(cols == rows + ns, 1.0, aug)
    for p in range(ns):
        col = jnp.broadcast_to(aug[:, p:p + 1], (ns, wide))
        inv = 1.0 / jnp.sqrt(jnp.broadcast_to(col[p:p + 1, :], (ns, wide)))
        top = jnp.broadcast_to(aug[p:p + 1, :], (ns, wide)) * inv
        aug = jnp.where(rows == p, top, jnp.where(rows > p, aug - (col * inv) * top, aug))
    r_ref[...] = jnp.where(cols >= rows, aug, 0.0)[:, :ns]

    unfold = (iota((wide, wide), 0) == ns + iota((wide, wide), 1) // T).astype(jnp.float32)
    mix = jnp.dot(aug, unfold, precision=HIGHEST, preferred_element_type=jnp.float32)
    mix = jnp.broadcast_to(mix[:, None, :], (ns, T, wide)).reshape(wide, wide)
    mix = jnp.where(same_row(wide, wide), mix, 0.0)

    def solve(i, carry):
        x = i // nyg
        y0 = pl.multiple_of((i % nyg) * T, T)
        d = jnp.dot(mix, wres[i], precision=HIGHEST, preferred_element_type=jnp.float32)
        dir_ref[:, x, pl.ds(y0, T), :] = d.reshape(ns, T, nz)
        return carry

    lax.fori_loop(0, cells, solve, 0)

    for c in range(chunks):
        part_copy(c).wait_send()
        fwd_copy(c).wait_send()
    for e in range(2):
        for f in range(nf):
            y_copy(e, f).wait_send()

    @pl.when(edge_chip)
    def _():
        for c in range(chunks):
            z_copy(c).wait_send()
    all_sum_sent(pa, pb, pa_s, pa_r, pb_s, pb_r)
    all_sum_sent(ga, gb, ga_s, ga_r, gb_s, gb_r)


def on_device(velocity, basis, mean_flow, shear):
    nf, nx, ny, nz = velocity.shape
    nk = basis.shape[0]
    groups = lax.axis_size("slab") // 4
    ns = 2 * nf
    cells = nx * ny // T
    f32, bf16 = jnp.float32, jnp.bfloat16
    chunks = 2 * nf * nx
    dma = pltpu.SemaphoreType.DMA
    vmem = pl.BlockSpec(memory_space=pltpu.VMEM)
    scratch = [
        pltpu.VMEM((nk, nx, ny, nz), bf16),
        pltpu.VMEM((nf, nx, ny, nz), f32),
        pltpu.VMEM((2, 3, nf, nx, ny, nz), f32),
        pltpu.VMEM((2, nf, nx, 8, nz), f32),
        pltpu.VMEM((nx, ny + 16, nz), f32),
        pltpu.VMEM((2, ny, nz), f32),
        pltpu.VMEM((nf, nx, ny, nz), f32),
        pltpu.VMEM((2, cells, nf * T, nz), bf16),
        pltpu.VMEM((2, nk, nf * T), f32),
        pltpu.VMEM((nk // T, ns * T, T * T), bf16),
        pltpu.VMEM((cells, ns * T, nz), f32),
        pltpu.VMEM((8, ns, nk), f32),
        pltpu.VMEM((groups, ns, nk), f32),
        pltpu.VMEM((8, ns, ns * T), f32),
        pltpu.VMEM((groups, ns, ns * T), f32),
        dma,
        *([dma((chunks,))] * 6),
        *([dma((2 * nf,))] * 2),
        *([dma((8,))] * 2),
        *([dma((groups,))] * 2),
        *([dma((8,))] * 2),
        *([dma((groups,))] * 2),
    ]
    advanced, coeffs, rfactor, directions = pl.pallas_call(
        functools.partial(kernel, groups),
        out_shape=[
            jax.ShapeDtypeStruct((nf, nx, ny, nz), f32),
            jax.ShapeDtypeStruct((ns, nk), f32),
            jax.ShapeDtypeStruct((ns, ns), f32),
            jax.ShapeDtypeStruct((ns, nx, ny, nz), f32),
        ],
        in_specs=[vmem, pl.BlockSpec(memory_space=pl.ANY), vmem, vmem],
        out_specs=[vmem] * 4,
        scratch_shapes=scratch,
        compiler_params=pltpu.CompilerParams(
            collective_id=0, has_side_effects=True, vmem_limit_bytes=48 * 1024 * 1024
        ),
    )(velocity, basis, mean_flow.reshape(1, -1), shear.reshape(1, -1))
    return advanced, coeffs.T, rfactor, directions


def solution(mesh):
    return jax.shard_map(
        on_device,
        mesh=mesh,
        in_specs=(P(None, "slab", "role", None), P(None, "slab", "role", None), P(), P()),
        out_specs=(P(None, "slab", "role", None), P(), P(), P(None, "slab", "role", None)),
        check_vma=False,
    )
```

time: 183 us -> 94.5 us (0.52)
  Pallas kernels: 0 us -> 88.3 us
  blocking collectives: 78.1 us -> 0 us
  matrix products: 32.2 us -> 0 us
  starting transfers between devices: 21.5 us -> 0 us
  local copies, waits for them, and re-layouts: 25.1 us -> 5.3 us
  waiting for transfers between devices: 12.2 us -> 0 us
  other arithmetic: 12 us -> 0 us
    pallas_call x0 -> x1, Pallas kernels: none -> 88.3 us  [on_device(): pl.pallas_call(functools.partial(kernel, groups), out_shape=[jax.ShapeDty...]
    psum x2 -> x0, blocking collectives: 78.1 us -> none  [the longest x1 40.3 us: on_device(): total_gram = lax.psum(local_gram, ('role', 'slab'))]
    dot_general x3 -> x0, matrix products: 31.2 us -> none  [the longest x1 20.8 us: on_device(): jnp.einsum('km,sm->ks', basis_rows, snaps_bf, preferred_element_type=jnp....]
    ppermute x8 -> x0, starting transfers between devices: 21.5 us -> none  [the longest x4 10.8 us: extended(): lax.ppermute(tail, axis, [(i, (i + 1) % count) for i in range(ends)])]
    unnamed x11 -> x10, local copies, waits for them, and re-layouts: 23.6 us -> 5.3 us
    ppermute x8 -> x0, waiting for transfers between devices: 12.2 us -> none  [the longest x4 10.3 us: extended(): lax.ppermute(tail, axis, [(i, (i + 1) % count) for i in range(ends)])]
    add x4 -> x0, other arithmetic: 7.04 us -> none  [the longest x2 4.51 us: stencil(): result = -profile * first_x + viscosity * laplace]
    another operation x5 -> x0, other arithmetic: 2.67 us -> none  [the longest x3 1.39 us: on_device(): lower_factor = jnp.linalg.cholesky(total_gram)]
  transfers between devices with their start and end apart: 8 -> 0, of which waited for: 3 -> 0; matrix products, arithmetic and copies ran while one was open for 12% -> 0% of each run, Pallas kernels for 0% -> 0%
where the time goes in v1:
time: 94.5 us; the launch traced here: 94.3 us
  Pallas kernels  88.3 us (93%)
  local copies, waits for them, and re-layouts  5.3 us (6%)
    pallas_call x1, Pallas kernels, on_device(): pl.pallas_call(functools.partial(kernel, groups), out_shape=[jax.ShapeDty...  88.3 us
    unnamed x10, local copies, waits for them, and re-layouts  5.3 us

profile of v1, /device:TPU:0, one launch (start us, length us, event | category | flops | bytes accessed | tf_op | source)
XLA Modules:
  0.0 94.3 jit_solution(4722312299085315381)
XLA Ops:
  0.6 0.0 copy-start
  0.6 1.0 %copy-done = f32[4,2,64,256]{3,2,1,0:T(8,128)S(1)} copy-done((f32[4,2,64,256]{3,2,1,0:T(8,128)S(1)}, f32[4,2,64,256]{3,2,1,0:T(8,128)}, u32[]{:S(2)}) %copy-start) | copy-done | bytes 524312
  1.7 0.0 copy-start.1
  1.7 0.7 copy-done.1
  2.3 0.0 copy-start.2
  2.3 0.7 copy-done.2
  3.0 88.3 %shard_map.75 = (f32[4,2,64,256]{3,2,1,0:T(8,128)S(1)}, f32[8,256]{1,0:T(8,128)S(1)}, f32[8,8]{1,0:T(8,128)S(1)}, f32[8,2,64,256]{3,2,1,0:T(8,128)S(1)}) custom-call(f32[4,2,64,256]{3,2,1,0:T(8,128)S(1)} %copy-done, bf16[256,2,64,256]{3,2,1,0:T(8,128)(2,1)} %basis_ref.1, f32[1,128]{1,0:T(1,128)S(1)} %bitcast.4, f32[1,128]{1,0:T(1,128)S(1)} %bitcast.5), custom_call_target="tpu_custom_call" | custom-call | tf_op jit(solution)/shard_map/pallas_call | solution.py:346
  91.3 0.8 copy.12
  92.1 0.6 copy.13
  92.7 0.6 copy.14
  93.3 1.0 %copy.15 = f32[8,2,64,256]{3,2,1,0:T(8,128)} copy(f32[8,2,64,256]{3,2,1,0:T(8,128)S(1)} %get-tuple-element.19) | data formatting | bytes 2097152
Async XLA Ops:
  0.6 1.0 %copy-start = (f32[4,2,64,256]{3,2,1,0:T(8,128)S(1)}, f32[4,2,64,256]{3,2,1,0:T(8,128)}, u32[]{:S(2)}) copy-start(f32[4,2,64,256]{3,2,1,0:T(8,128)} %v_ref.1) | copy-start | bytes 1572868
  1.7 0.7 copy-start.1
  2.3 0.7 copy-start.2

commit v2 on v1

--- a/solution.py
+++ b/solution.py
@@ -28,11 +28,12 @@
     )
 
 
-def kernel(groups, v_ref, basis_ref, flow_ref, shear_ref,
+def kernel(groups, v_hbm, basis_ref, flow_hbm, shear_hbm,
            adv_ref, coef_ref, r_ref, dir_ref,
+           v_ref, flow_ref, shear_ref, rep16,
            bas, s1, halo, yh, yx, prof, tend, sbf, racc, cbig, wres,
            pa, pb, ga, gb,
-           bas_sem, part_s, part_r, fwd_s, fwd_r, z_s, z_r, y_s, y_r,
+           in_sem, bas_sem, part_s, part_r, fwd_s, fwd_r, z_s, z_r, y_s, y_r,
            pa_s, pa_r, pb_s, pb_r, ga_s, ga_r, gb_s, gb_r):
     nf, nx, ny, nz = v_ref.shape
     nk = bas.shape[0]
@@ -50,6 +51,10 @@
     rslot = (j % 2) * (1 + j // 2)
     me8 = role * 4 + j
 
+    small = [(v_hbm, v_ref), (flow_hbm, flow_ref), (shear_hbm, shear_ref)]
+    loads = [pltpu.make_async_copy(src, dst, in_sem.at[i]) for i, (src, dst) in enumerate(small)]
+    for load in loads:
+        load.start()
     basis_copy = pltpu.make_async_copy(basis_ref, bas, bas_sem)
     basis_copy.start()
 
@@ -64,6 +69,8 @@
         group_peers.append((p, (role, p * 4 + j)))
     for _, dev in plane_peers + group_peers:
         pl.semaphore_signal(barrier, inc=1, device_id=dev, device_id_type=MESH)
+    for load in loads:
+        load.wait()
     pl.semaphore_wait(barrier, 6 + groups)
 
     def remote(src, dst, ss, rs, dev):
@@ -72,6 +79,7 @@
         )
 
     chunks = 2 * nf * nx
+    window, fwd_lag, z_lag = 4, 2, 4
 
     def where_of(c):
         e, rest = divmod(c, nf * nx)
@@ -97,7 +105,7 @@
         i = e * nf + f
         return remote(src, yh.at[e, f], y_s.at[i], y_r.at[i], (1 - role, slab))
 
-    for c in range(nf * nx):
+    for c in range(window):
         part_copy(c).start()
     for f in range(nf):
         y_copy(0, f).start()
@@ -107,6 +115,8 @@
     for i, ref in enumerate((flow_ref, shear_ref)):
         col = jnp.sum(jnp.where(pick, ref[...], 0.0), axis=1, keepdims=True)
         prof[i] = jnp.broadcast_to(col, (ny, nz))
+    spot = iota((nk, T * T), 0) % T == iota((nk, T * T), 1) // T
+    rep16[...] = spot.astype(jnp.float32).astype(jnp.bfloat16)
     role_f = role.astype(jnp.float32)
 
     def tendency(e, f):
@@ -150,23 +160,25 @@
         def body(kb, carry):
             project(half, kb)
             return carry
-        lax.fori_loop(lo, hi, body, 0)
+        lax.fori_loop(lo, hi, body, 0, unroll=2)
 
     nkb = nk // T
     edge_chip = j % 3 == 0
     done_kb = 0
-    for t in range(chunks + 2):
+    for t in range(chunks + z_lag):
         if t < chunks:
             part_copy(t).wait_recv()
             fwd_copy(t).start()
-        if 0 <= t - 1 < chunks:
-            fwd_copy(t - 1).wait_recv()
+            if t + window < nf * nx:
+                part_copy(t + window).start()
+        if 0 <= t - fwd_lag < chunks:
+            fwd_copy(t - fwd_lag).wait_recv()
 
             @pl.when(edge_chip)
             def _():
-                z_copy(t - 1).start()
-        if t - 2 >= 0:
-            c = t - 2
+                z_copy(t - fwd_lag).start()
+        if t - z_lag >= 0:
+            c = t - z_lag
 
             @pl.when(edge_chip)
             def _():
@@ -191,11 +203,11 @@
                         )
                         adv_ref[f, xx] = val
                         keep_rounded(1, f, xx, val)
-        first = nf * nx + 2
+        first = nf * nx + z_lag
         if t >= first:
             if t == first:
                 basis_copy.wait()
-            upto = ((t - first + 1) * nkb) // (chunks + 2 - first)
+            upto = ((t - first + 1) * nkb) // (chunks + z_lag - first)
             project_range(0, done_kb, upto)
             done_kb = upto
     project_range(1, 0, nkb)
@@ -237,15 +249,15 @@
 
     ns = 2 * nf
 
-    def spread(kb, carry):
-        rep = (iota((nk, T * T), 0) == kb * T + iota((nk, T * T), 1) // T)
-        rep = rep.astype(jnp.float32).astype(jnp.bfloat16)
-        row = jnp.dot(cb, rep, preferred_element_type=jnp.float32)
+    tall = jnp.broadcast_to(cb.astype(jnp.float32)[None], (nkb, ns, nk)).reshape(nkb * ns, nk)
+    own = iota((nkb * ns, nk), 0) // ns == iota((nkb * ns, nk), 1) // T
+    tall = jnp.where(own, tall, 0.0).astype(jnp.bfloat16)
+    lanes = jnp.dot(tall, rep16[...], preferred_element_type=jnp.float32)
+    keep = same_row(ns * T, T * T)
+    for kb in range(nkb):
+        row = lanes[kb * ns:(kb + 1) * ns, :]
         full = jnp.broadcast_to(row[:, None, :], (ns, T, T * T)).reshape(ns * T, T * T)
-        cbig[kb] = jnp.where(same_row(ns * T, T * T), full, 0.0).astype(jnp.bfloat16)
-        return carry
-
-    lax.fori_loop(0, nkb, spread, 0)
+        cbig[kb] = jnp.where(keep, full, 0.0).astype(jnp.bfloat16)
 
     def residual(i, gram):
         x = i // nyg
@@ -263,7 +275,7 @@
         wres[i] = w
         return gram + nt_dot(w, w, HIGHEST)
 
-    gram = lax.fori_loop(0, cells, residual, jnp.zeros((ns * T, ns * T), jnp.float32))
+    gram = lax.fori_loop(0, cells, residual, jnp.zeros((ns * T, ns * T), jnp.float32), unroll=2)
     gram = jnp.where(same_row(ns * T, ns * T), gram, 0.0)
     gram = jnp.sum(gram.reshape(ns, T, ns * T), axis=1)
     gram = all_sum(gram, ga, gb, ga_s, ga_r, gb_s, gb_r)
@@ -292,7 +304,7 @@
         dir_ref[:, x, pl.ds(y0, T), :] = d.reshape(ns, T, nz)
         return carry
 
-    lax.fori_loop(0, cells, solve, 0)
+    lax.fori_loop(0, cells, solve, 0, unroll=4)
 
     for c in range(chunks):
         part_copy(c).wait_send()
@@ -320,6 +332,10 @@
     dma = pltpu.SemaphoreType.DMA
     vmem = pl.BlockSpec(memory_space=pltpu.VMEM)
     scratch = [
+        pltpu.VMEM((nf, nx, ny, nz), f32),
+        pltpu.VMEM((1, mean_flow.shape[0]), f32),
+        pltpu.VMEM((1, shear.shape[0]), f32),
+        pltpu.VMEM((nk, T * T), bf16),
         pltpu.VMEM((nk, nx, ny, nz), bf16),
         pltpu.VMEM((nf, nx, ny, nz), f32),
         pltpu.VMEM((2, 3, nf, nx, ny, nz), f32),
@@ -335,6 +351,7 @@
         pltpu.VMEM((groups, ns, nk), f32),
         pltpu.VMEM((8, ns, ns * T), f32),
         pltpu.VMEM((groups, ns, ns * T), f32),
+        dma((3,)),
         dma,
         *([dma((chunks,))] * 6),
         *([dma((2 * nf,))] * 2),
@@ -351,11 +368,11 @@
             jax.ShapeDtypeStruct((ns, ns), f32),
             jax.ShapeDtypeStruct((ns, nx, ny, nz), f32),
         ],
-        in_specs=[vmem, pl.BlockSpec(memory_space=pl.ANY), vmem, vmem],
+        in_specs=[pl.BlockSpec(memory_space=pl.ANY)] * 4,
         out_specs=[vmem] * 4,
         scratch_shapes=scratch,
         compiler_params=pltpu.CompilerParams(
-            collective_id=0, has_side_effects=True, vmem_limit_bytes=48 * 1024 * 1024
+            collective_id=0, has_side_effects=True, vmem_limit_bytes=60 * 1024 * 1024
         ),
     )(velocity, basis, mean_flow.reshape(1, -1), shear.reshape(1, -1))
     return advanced, coeffs.T, rfactor, directions

time: 94.5 us -> 78.3 us (0.83)
  Pallas kernels: 88.3 us -> 70.6 us
  local copies, waits for them, and re-layouts: 5.3 us -> 6.72 us
    pallas_call x1, Pallas kernels: 88.3 us -> 70.6 us  [on_device(): pl.pallas_call(functools.partial(kernel, groups), out_shape=[jax.ShapeDty...]
    unnamed x10 -> x4, local copies, waits for them, and re-layouts: 5.3 us -> 6.72 us
where the time goes in v2:
time: 78.3 us; the launch traced here: 78 us
  Pallas kernels  70.6 us (90%)
  local copies, waits for them, and re-layouts  6.72 us (9%)
    pallas_call x1, Pallas kernels, on_device(): pl.pallas_call(functools.partial(kernel, groups), out_shape=[jax.ShapeDty...  70.6 us
    unnamed x4, local copies, waits for them, and re-layouts  6.72 us

profile of v2, /device:TPU:0, one launch (start us, length us, event | category | flops | bytes accessed | tf_op | source)
XLA Modules:
  0.0 78.0 jit_solution(11728347006963231568)
XLA Ops:
  0.6 70.6 %shard_map.75 = (f32[4,2,64,256]{3,2,1,0:T(8,128)}, f32[8,256]{1,0:T(8,128)}, f32[8,8]{1,0:T(8,128)}, f32[8,2,64,256]{3,2,1,0:T(8,128)}) custom-call(f32[4,2,64,256]{3,2,1,0:T(8,128)} %v_hbm.1, bf16[256,2,64,256]{3,2,1,0:T(8,128)(2,1)} %basis_ref.1, f32[1,128]{1,0:T(1,128)} %bitcast.4, f32[1,128]{1,0:T(1,128)} %bitcast.5), custom_call_target="tpu_custom_call" | custom-call | tf_op jit(solution)/shard_map/pallas_call | solution.py:363
  71.3 1.9 %copy.12 = f32[4,2,64,256]{3,2,1,0:T(8,128)} copy(f32[4,2,64,256]{3,2,1,0:T(8,128)} %get-tuple-element.16) | data formatting | bytes 1048576
  73.1 1.3 %copy.13 = f32[256,8]{0,1:T(8,128)} copy(f32[256,8]{0,1:T(8,128)} %bitcast.3) | data formatting | bytes 16384
  74.4 1.3 %copy.14 = f32[8,8]{1,0:T(8,128)} copy(f32[8,8]{1,0:T(8,128)} %get-tuple-element.18) | data formatting | bytes 512
  75.7 2.3 %copy.15 = f32[8,2,64,256]{3,2,1,0:T(8,128)} copy(f32[8,2,64,256]{3,2,1,0:T(8,128)} %get-tuple-element.19) | data formatting | bytes 2097152

commit v3 on v2

--- a/solution.py
+++ b/solution.py
@@ -29,9 +29,9 @@
 
 
 def kernel(groups, v_hbm, basis_ref, flow_hbm, shear_hbm,
-           adv_ref, coef_ref, r_ref, dir_ref,
+           adv_ref, coef_ref, r_ref, mix_ref, wres,
            v_ref, flow_ref, shear_ref, rep16,
-           bas, s1, halo, yh, yx, prof, tend, sbf, racc, cbig, wres,
+           bas, s1, halo, yh, yx, prof, tend, sbf, racc, cbig,
            pa, pb, ga, gb,
            in_sem, bas_sem, part_s, part_r, fwd_s, fwd_r, z_s, z_r, y_s, y_r,
            pa_s, pa_r, pb_s, pb_r, ga_s, ga_r, gb_s, gb_r):
@@ -295,16 +295,7 @@
     unfold = (iota((wide, wide), 0) == ns + iota((wide, wide), 1) // T).astype(jnp.float32)
     mix = jnp.dot(aug, unfold, precision=HIGHEST, preferred_element_type=jnp.float32)
     mix = jnp.broadcast_to(mix[:, None, :], (ns, T, wide)).reshape(wide, wide)
-    mix = jnp.where(same_row(wide, wide), mix, 0.0)
-
-    def solve(i, carry):
-        x = i // nyg
-        y0 = pl.multiple_of((i % nyg) * T, T)
-        d = jnp.dot(mix, wres[i], precision=HIGHEST, preferred_element_type=jnp.float32)
-        dir_ref[:, x, pl.ds(y0, T), :] = d.reshape(ns, T, nz)
-        return carry
-
-    lax.fori_loop(0, cells, solve, 0, unroll=4)
+    mix_ref[...] = jnp.where(same_row(wide, wide), mix, 0.0)
 
     for c in range(chunks):
         part_copy(c).wait_send()
@@ -319,6 +310,18 @@
             z_copy(c).wait_send()
     all_sum_sent(pa, pb, pa_s, pa_r, pb_s, pb_r)
     all_sum_sent(ga, gb, ga_s, ga_r, gb_s, gb_r)
+
+
+def finish(adv_in, coef_in, r_in, mix_ref, wres, adv_ref, coef_ref, r_ref, dir_ref):
+    ns, nx, ny, nz = dir_ref.shape
+    nyg = ny // T
+    adv_ref[...] = adv_in[...]
+    coef_ref[...] = coef_in[...]
+    r_ref[...] = r_in[...]
+    for i in range(nx * nyg):
+        x, y0 = i // nyg, (i % nyg) * T
+        d = jnp.dot(mix_ref[...], wres[i], precision=HIGHEST, preferred_element_type=jnp.float32)
+        dir_ref[:, x, y0:y0 + T, :] = d.reshape(ns, T, nz)
 
 
 def on_device(velocity, basis, mean_flow, shear):
@@ -346,7 +349,6 @@
         pltpu.VMEM((2, cells, nf * T, nz), bf16),
         pltpu.VMEM((2, nk, nf * T), f32),
         pltpu.VMEM((nk // T, ns * T, T * T), bf16),
-        pltpu.VMEM((cells, ns * T, nz), f32),
         pltpu.VMEM((8, ns, nk), f32),
         pltpu.VMEM((groups, ns, nk), f32),
         pltpu.VMEM((8, ns, ns * T), f32),
@@ -360,21 +362,34 @@
         *([dma((8,))] * 2),
         *([dma((groups,))] * 2),
     ]
+    results = pl.pallas_call(
+        functools.partial(kernel, groups),
+        out_shape=[
+            jax.ShapeDtypeStruct((nf, nx, ny, nz), f32),
+            jax.ShapeDtypeStruct((ns, nk), f32),
+            jax.ShapeDtypeStruct((ns, ns), f32),
+            jax.ShapeDtypeStruct((ns * T, ns * T), f32),
+            jax.ShapeDtypeStruct((cells, ns * T, nz), f32),
+        ],
+        in_specs=[pl.BlockSpec(memory_space=pl.ANY)] * 4,
+        out_specs=[vmem] * 5,
+        scratch_shapes=scratch,
+        compiler_params=pltpu.CompilerParams(
+            collective_id=0, has_side_effects=True, vmem_limit_bytes=48 * 1024 * 1024
+        ),
+    )(velocity, basis, mean_flow.reshape(1, -1), shear.reshape(1, -1))
     advanced, coeffs, rfactor, directions = pl.pallas_call(
-        functools.partial(kernel, groups),
+        finish,
         out_shape=[
             jax.ShapeDtypeStruct((nf, nx, ny, nz), f32),
             jax.ShapeDtypeStruct((ns, nk), f32),
             jax.ShapeDtypeStruct((ns, ns), f32),
             jax.ShapeDtypeStruct((ns, nx, ny, nz), f32),
         ],
-        in_specs=[pl.BlockSpec(memory_space=pl.ANY)] * 4,
+        in_specs=[vmem] * 5,
         out_specs=[vmem] * 4,
-        scratch_shapes=scratch,
-        compiler_params=pltpu.CompilerParams(
-            collective_id=0, has_side_effects=True, vmem_limit_bytes=60 * 1024 * 1024
-        ),
-    )(velocity, basis, mean_flow.reshape(1, -1), shear.reshape(1, -1))
+        compiler_params=pltpu.CompilerParams(vmem_limit_bytes=16 * 1024 * 1024),
+    )(*results)
     return advanced, coeffs.T, rfactor, directions
 
 

time: 78.3 us -> 73.4 us (0.937)
  local copies, waits for them, and re-layouts: 6.72 us -> 2.34 us
    unnamed x4 -> x6, local copies, waits for them, and re-layouts: 6.72 us -> 2.34 us
    pallas_call x1, Pallas kernels: 70.6 us -> 68.2 us  [on_device(): pl.pallas_call(functools.partial(kernel, groups), out_shape=[jax.ShapeDty...]
    pallas_call x0 -> x1, Pallas kernels: none -> 2.02 us  [on_device(): pl.pallas_call(finish, out_shape=[jax.ShapeDtypeStruct((nf, nx, ny, nz),...]
where the time goes in v3:
time: 73.4 us; the launch traced here: 73.3 us
  Pallas kernels  70.3 us (96%)
  local copies, waits for them, and re-layouts  2.34 us (3%)
    pallas_call x1, Pallas kernels, on_device(): pl.pallas_call(functools.partial(kernel, groups), out_shape=[jax.ShapeDty...  68.2 us
    unnamed x6, local copies, waits for them, and re-layouts  2.34 us
    pallas_call x1, Pallas kernels, on_device(): pl.pallas_call(finish, out_shape=[jax.ShapeDtypeStruct((nf, nx, ny, nz),...  2.02 us

profile of v3, /device:TPU:0, one launch (start us, length us, event | category | flops | bytes accessed | tf_op | source)
XLA Modules:
  0.0 73.3 jit_solution(16678329161425196117)
XLA Ops:
  0.6 0.0 copy-start
  0.6 1.0 %copy-done = f32[4,2,64,256]{3,2,1,0:T(8,128)S(1)} copy-done((f32[4,2,64,256]{3,2,1,0:T(8,128)S(1)}, f32[4,2,64,256]{3,2,1,0:T(8,128)}, u32[]{:S(2)}) %copy-start) | copy-done | bytes 524312
  1.7 0.0 copy-start.1
  1.7 0.7 copy-done.1
  2.3 0.0 copy-start.2
  2.3 0.7 copy-done.2
  3.0 68.2 %shard_map.75 = (f32[4,2,64,256]{3,2,1,0:T(8,128)S(1)}, f32[8,256]{1,0:T(8,128)S(1)}, f32[8,8]{1,0:T(8,128)S(1)}, f32[128,128]{1,0:T(8,128)S(1)}, f32[8,128,256]{2,1,0:T(8,128)S(1)}) custom-call(f32[4,2,64,256]{3,2,1,0:T(8,128)S(1)} %copy-done, bf16[256,2,64,256]{3,2,1,0:T(8,128)(2,1)} %basis_ref.1, f32[1,128]{1,0:T(1,128)S(1)} %bitcast.3, f32[1,128]{1,0:T(1,128)S(1)} %bitcast.4), custom_call_target="tpu_custom_call" | custom-call | tf_op jit(solution)/shard_map/pallas_call | solution.py:365
  71.2 2.0 %shard_map.76 = (f32[4,2,64,256]{3,2,1,0:T(8,128)}, f32[8,256]{1,0:T(8,128)}, f32[8,8]{1,0:T(8,128)}, f32[8,2,64,256]{3,2,1,0:T(8,128)}) custom-call(f32[4,2,64,256]{3,2,1,0:T(8,128)S(1)} %get-tuple-element.13.adv_in, f32[8,256]{1,0:T(8,128)S(1)} %get-tuple-element.14.coef_in, f32[8,8]{1,0:T(8,128)S(1)} %get-tuple-element.15.r_in, ...), custom_call_target="tpu_custom_call" | custom-call | tf_op jit(solution)/shard_map/pallas_call | solution.py:381
Async XLA Ops:
  0.6 1.0 %copy-start = (f32[4,2,64,256]{3,2,1,0:T(8,128)S(1)}, f32[4,2,64,256]{3,2,1,0:T(8,128)}, u32[]{:S(2)}) copy-start(f32[4,2,64,256]{3,2,1,0:T(8,128)} %v_hbm.1) | copy-start | bytes 1572868
  1.7 0.7 copy-start.1
  2.3 0.7 copy-start.2
